TPU v7x, 256 devices: a whole 4x4x8 slice. The times are simulated.
256 devices in a mesh: row: 8 (over x_lo, y), col: 16 (over z, x_hi), pole: 2 (over core).
Axes of the slice: x: 4 (x_hi: 2, x_lo: 2; x = x_hi * 2 + x_lo), y: 4, z: 8, core: 2. Of those that a mesh axis runs over, the one named last changes fastest.
Arguments:
- ainv: bfloat16 [2, 2, 10240, 10240], P('pole', None, 'row', 'col'), may hold values from -0.0625 to 0.0625
- pattern: int32 [80, 80], P('row', 'col'), may hold values from 0 to 1, as said below
- rows_a: int32 [80], P('col'), may hold values 0 or 1
- rows_b: int32 [80], P('col'), may hold values 0 or 1
- panel_a: bfloat16 [2, 2, 256, 10240], P('pole', None, 'row', 'col'), may hold values from -6 to 6
- panel_b: bfloat16 [2, 2, 256, 10240], P('pole', None, 'row', 'col'), may hold values from -6 to 6
- tri_inv_a: bfloat16 [2, 2, 256, 256], P('pole'), may hold values from -0.375 to 0.375
- tri_inv_b: bfloat16 [2, 2, 256, 256], P('pole'), may hold values from -0.375 to 0.375
- cross_b: bfloat16 [2, 2, 256, 256], P('pole'), may hold values from -0.375 to 0.375
- weights: float32 [2, 2], P('pole'), may hold values from -4 to 4
Outputs:
- dens_a: float32 [10240, 256], P(('row', 'col'), 'pole')
- dens_b: float32 [10240, 256], P(('row', 'col'), 'pole')
Inputs may be any that keep to these rules, and one draw needn't show every extreme that they name: 1 marks a selected block of the ancestor inverse, 0 a block outside the pattern; the share of selected blocks differs between block rows. `rows_a`: 1 marks an ancestor block row in the first supernode's structure. `rows_b`: 1 marks an ancestor block row in the second supernode's structure.
All inputs are finite; a program needn't handle non-finite values.
Results may differ from a plain program's by a relative error of at most 0.02.
Values may be sent and summed in bfloat16 or wider, within the bound.
A program may use at most 64 MiB of HBM per device.

v0:
```python
import jax
import jax.numpy as jnp
from jax import lax
from jax.sharding import PartitionSpec as P

W = 256
BS = 128


def keep_rows(panel, rows):
    shaped = panel.reshape(2, panel.shape[1], rows.shape[0], BS)
    shaped = shaped * rows[None, None, :, None].astype(jnp.bfloat16)
    return shaped.reshape(2, panel.shape[1], panel.shape[2])


def complex_grid(tri):
    return jnp.stack([jnp.stack([tri[0], -tri[1]]), jnp.stack([tri[1], tri[0]])])


def scale_rows(grid, lower_rows):
    return jnp.einsum("dcwo,cwr->dor", grid, lower_rows, preferred_element_type=jnp.float32).astype(
        jnp.bfloat16
    )


def operand_pair(lhat):
    return jnp.stack([jnp.stack([lhat[0], lhat[1]]), jnp.stack([-lhat[1], lhat[0]])])


def block_product(masked, pair, row_count):
    result = jnp.einsum("crk,cdok->rdo", masked, pair, preferred_element_type=jnp.float32)
    return result.reshape(row_count, -1)


def per_device(
    ainv, pattern, rows_a, rows_b, panel_a, panel_b, tri_inv_a, tri_inv_b, cross_b, weights
):
    tile_rows = ainv.shape[2]
    tile_cols = ainv.shape[3]
    masked = ainv[0].reshape(2, tile_rows // BS, BS, tile_cols // BS, BS) * pattern[
        None, :, None, :, None
    ].astype(jnp.bfloat16)
    masked = masked.reshape(2, tile_rows, tile_cols)
    lower_a = keep_rows(panel_a[0], rows_a)
    lower_b = keep_rows(panel_b[0], rows_b)
    full_a, full_b = (
        lax.all_gather(lower_a, "row", axis=1, tiled=True),
        lax.all_gather(lower_b, "row", axis=1, tiled=True),
    )
    grid_a = complex_grid(tri_inv_a[0])
    grid_b = complex_grid(tri_inv_b[0])
    lhat_a = scale_rows(grid_a, full_a)
    lhat_b = scale_rows(grid_b, full_b)
    pair_a = operand_pair(lhat_a)
    pair_b = operand_pair(lhat_b)
    cross_hat = jnp.einsum(
        "dcwo,caw->dao", grid_b, cross_b[0], preferred_element_type=jnp.float32
    ).astype(jnp.bfloat16)
    coupling = jnp.concatenate(
        [
            jnp.concatenate([cross_hat[0], cross_hat[1]], 1),
            jnp.concatenate([-cross_hat[1], cross_hat[0]], 1),
        ],
        0,
    ).astype(jnp.float32)
    w_real = weights[0, 0]
    w_imag = weights[0, 1]
    out_rows = tile_rows // lax.axis_size("col")
    summed_a = lax.psum_scatter(
        block_product(masked, pair_a, out_rows * lax.axis_size("col")).astype(jnp.bfloat16),
        "col",
        scatter_dimension=0,
        tiled=True,
    ).astype(jnp.float32)
    summed_b = lax.psum_scatter(
        block_product(masked, pair_b, out_rows * lax.axis_size("col")).astype(jnp.bfloat16),
        "col",
        scatter_dimension=0,
        tiled=True,
    ).astype(jnp.float32)
    update_a = -summed_a
    update_b = -summed_b - jnp.dot(update_a, coupling, precision=lax.Precision.HIGHEST)
    term_a = w_real * update_a[:, W:] + w_imag * update_a[:, :W]
    term_b = w_real * update_b[:, W:] + w_imag * update_b[:, :W]
    dens_a, dens_b = (
        lax.psum_scatter(
            term_a.astype(jnp.bfloat16), "pole", scatter_dimension=1, tiled=True
        ).astype(jnp.float32),
        lax.psum_scatter(
            term_b.astype(jnp.bfloat16), "pole", scatter_dimension=1, tiled=True
        ).astype(jnp.float32),
    )
    return (dens_a, dens_b)


def solution(mesh):
    placed = (
        P("pole", None, "row", "col"),
        P("row", "col"),
        P("col"),
        P("col"),
        P("pole", None, "row", "col"),
        P("pole", None, "row", "col"),
        P("pole", None, None, None),
        P("pole", None, None, None),
        P("pole", None, None, None),
        P("pole", None),
    )
    return jax.shard_map(
        per_device,
        mesh=mesh,
        in_specs=placed,
        out_specs=(P(("row", "col"), "pole"), P(("row", "col"), "pole")),
        check_vma=False,
    )
```

profile of v0, /device:TPU:1, one launch (start us, length us, event | category | flops | bytes accessed | tf_op | source)
XLA Modules:
  0.0 498.7 jit_solution(8722613564725677555)
XLA Ops:
  7.2 0.0 copy-start
  7.2 0.0 reduce-scatter.9.cloned.1.call-start
  7.2 0.7 convert_element_type.49
  7.9 0.1 copy.22
  8.0 0.4 mul.64
  8.5 0.0 copy-start.8
  8.5 0.0 copy-start.3
  8.5 0.0 copy-start.1
  8.5 0.4 copy.40
  8.9 0.2 copy-done.8
  9.1 0.1 broadcast_bitcast_fusion.1
  9.2 0.2 copy-done.3
  9.4 24.9 %all_gather.6 = bf16[2,256,640]{2,1,0:T(8,128)(2,1)S(1)} all-gather(bf16[2,32,640]{2,1,0:T(8,128)(2,1)S(1)} %bitcast_multiply_fusion.1), channel_id=1, replica_groups=mesh['row'=8,'col'=16,'pole'=2] {'row'}, dimensions={1}, use_global_device_ids=true | all-gather | bytes 737280 | tf_op jit(solution)/shard_map/all_gather | solution.py:47
  34.3 0.0 copy-done.1
  34.4 0.1 copy.35
  34.5 0.1 copy.34
  34.6 0.6 fusion.20
  35.2 0.1 slice_negate_fusion.1
  35.3 0.0 copy-start.6
  35.3 0.1 maximum_bitcast_fusion
  35.4 0.1 pad_maximum_fusion
  35.5 1.7 copy-done.6
  37.2 3.0 fusion.13
  40.2 0.0 copy-start.2
  40.3 0.0 copy-start.9
  40.3 0.0 reduce-scatter.9.cloned.1.call-update
  40.3 0.0 copy-start.4
  40.3 0.0 reduce-scatter.11.cloned.1.call-start
  40.3 0.9 copy-done.2
  41.2 0.1 copy.37
  41.3 0.1 copy.36
  41.4 0.0 copy-done.9
  41.5 0.1 broadcast_bitcast_fusion
  41.6 0.0 copy-done.4
  41.6 23.8 %all_gather.7 = bf16[2,256,640]{2,1,0:T(8,128)(2,1)S(1)} all-gather(bf16[2,32,640]{2,1,0:T(8,128)(2,1)S(1)} %bitcast_multiply_fusion), channel_id=1, replica_groups=mesh['row'=8,'col'=16,'pole'=2] {'row'}, dimensions={1}, use_global_device_ids=true | all-gather | bytes 737280 | tf_op jit(solution)/shard_map/all_gather | solution.py:48
  65.4 0.6 fusion.21
  66.0 0.1 slice_negate_fusion
  66.0 0.0 copy-start.7
  66.0 0.1 maximum_bitcast_fusion.1
  66.1 0.1 pad_maximum_fusion.1
  66.3 1.7 copy-done.7
  68.0 3.0 fusion.10
  71.0 0.0 reduce-scatter.11.cloned.1.call-update
  71.0 0.0 reduce-scatter.13.cloned.1.call-start
  71.1 0.6 copy-done.5
  71.6 0.6 fusion.48
  72.2 0.0 copy-done
  72.2 0.3 fusion.23
  72.6 174.7 %reduce-scatter.9.cloned.1.call-done = bf16[80,512]{1,0:T(8,128)(2,1)} async-done(((bf16[1280,512]{1,0:T(8,128)(2,1)}), bf16[80,512]{1,0:T(8,128)(2,1)}) %reduce-scatter.9.cloned.1.call-update) | async-done | bytes 81936 | tf_op jit(solution)/shard_map/reduce_scatter | solution.py:69
  247.3 0.9 convert_negate_fusion
  248.2 205.7 %reduce-scatter.11.cloned.1.call-done = bf16[80,512]{1,0:T(8,128)(2,1)} async-done(((bf16[1280,512]{1,0:T(8,128)(2,1)}), bf16[80,512]{1,0:T(8,128)(2,1)}) %reduce-scatter.11.cloned.1.call-update) | async-done | bytes 81936 | tf_op jit(solution)/shard_map/reduce_scatter | solution.py:75
  453.9 1.5 convolution_subtract_fusion
  455.4 1.3 fusion.38
  456.8 0.7 copy.30
  457.5 0.0 reduce-scatter.13.cloned.1.call-update
  457.5 0.0 reduce-scatter.15.cloned.1.call-start
  457.6 0.7 copy.32
  458.3 0.0 reduce-scatter.15.cloned.1.call-update
  458.3 16.0 %reduce-scatter.13.cloned.1.call-done = bf16[128,80]{1,0:T(8,128)(2,1)} async-done(((bf16[256,80]{1,0:T(8,128)(2,1)}), bf16[128,80]{1,0:T(8,128)(2,1)}) %reduce-scatter.13.cloned.1.call-update) | async-done | bytes 20496
  474.3 0.8 copy.31
  475.1 0.6 convert_element_type.55
  475.8 14.9 %reduce-scatter.15.cloned.1.call-done = bf16[128,80]{1,0:T(8,128)(2,1)} async-done(((bf16[256,80]{1,0:T(8,128)(2,1)}), bf16[128,80]{1,0:T(8,128)(2,1)}) %reduce-scatter.15.cloned.1.call-update) | async-done | bytes 20496
  490.7 0.8 copy.33
  491.5 0.6 convert_element_type.63
  (13 shorter events, 0.2 us)
Async XLA Ops:
  7.2 65.1 %copy-start = (bf16[1,2,256,256]{3,2,1,0:T(8,128)(2,1)S(1)}, bf16[1,2,256,256]{3,2,1,0:T(8,128)(2,1)}, u32[]{:S(2)}) copy-start(bf16[1,2,256,256]{3,2,1,0:T(8,128)(2,1)} %param.18) | copy-start | bytes 786436
  7.2 240.2 %reduce-scatter.9.cloned.1.call-start = ((), (), s32[]{:S(2)}) async-start(), calls=%async_computation.4 | async-start | bytes 1392640 | tf_op jit(solution)/shard_map/reduce_scatter | solution.py:69
  8.5 0.7 copy-start.8
  8.5 0.9 copy-start.3
  8.5 25.8 %copy-start.1 = (bf16[1,2,256,256]{3,2,1,0:T(8,128)(2,1)S(1)}, bf16[1,2,256,256]{3,2,1,0:T(8,128)(2,1)}, u32[]{:S(2)}) copy-start(bf16[1,2,256,256]{3,2,1,0:T(8,128)(2,1)} %param.16) | copy-start | bytes 786436
  35.3 1.9 copy-start.6
  40.2 0.9 copy-start.2
  40.3 1.2 copy-start.9
  40.3 1.3 copy-start.4
  40.3 413.6 %reduce-scatter.11.cloned.1.call-start = ((), (), s32[]{:S(2)}) async-start(), calls=%async_computation.5 | async-start | bytes 1392640 | tf_op jit(solution)/shard_map/reduce_scatter | solution.py:75
  66.0 1.9 copy-start.7
  71.0 0.7 copy-start.5
  71.0 403.3 %reduce-scatter.13.cloned.1.call-start = ((), (), s32[]{:S(2)}) async-start(), calls=%async_computation.6 | async-start | bytes 98304
  457.5 33.2 %reduce-scatter.15.cloned.1.call-start = ((), (), s32[]{:S(2)}) async-start(), calls=%async_computation.7 | async-start | bytes 98304
Sparse Core Ops, SparseCore 0:
  40.4 206.8 reduce-scatter.8
  251.7 202.1 reduce-scatter.10
  457.6 16.5 reduce-scatter.12
  476.6 14.0 reduce-scatter.14
where the time goes:
time: 499 us
  waiting for transfers between devices  411 us (82%)
  blocking collectives  48.7 us (10%)
  between operations  14 us (3%)
  local copies, waits for them, and re-layouts  10.5 us (2%)
  matrix products  9.06 us (2%)
    reduce_scatter x1, waiting for transfers between devices, per_device(): lax.psum_scatter(block_product(masked, pair_b, out_rows * lax.axis_size('...  206 us
    reduce_scatter x1, waiting for transfers between devices, per_device(): lax.psum_scatter(block_product(masked, pair_a, out_rows * lax.axis_size('...  175 us
    unnamed x6, waiting for transfers between devices  30.9 us
    all_gather x1, blocking collectives, per_device(): lax.all_gather(lower_a, 'row', axis=1, tiled=True)  24.9 us
    all_gather x1, blocking collectives, per_device(): lax.all_gather(lower_b, 'row', axis=1, tiled=True)  23.8 us
  transfers between devices with their start and end apart: 4, of which 4 were waited for; matrix products, arithmetic and copies ran while one was open for 2% of the time, Pallas kernels for 0%

commit v1 on v0

v1 whole, which is shorter than its diff:
```python
import functools

import jax
import jax.numpy as jnp
from jax import lax
from jax.experimental import pallas as pl
from jax.experimental.pallas import tpu as pltpu
from jax.sharding import PartitionSpec as P

BS = 128
CHUNKS = 4
MESH = pl.DeviceIdType.MESH
NT = (((1,), (1,)), ((), ()))


def remote(src, dst, send, recv, where):
    return pltpu.make_async_remote_copy(
        src_ref=src,
        dst_ref=dst,
        send_sem=send,
        recv_sem=recv,
        device_id=where,
        device_id_type=MESH,
    )


def lane_marks(marks, count):
    return jnp.concatenate(
        [jnp.full((1, BS), marks(j), jnp.int32) for j in range(count)], axis=1
    ).astype(jnp.float32).astype(jnp.bfloat16)


def kernel(
    nrow,
    ncol,
    ainv,
    pattern,
    rows_a,
    rows_b,
    panel_a,
    panel_b,
    tri_a,
    tri_b,
    cross,
    weights,
    out_a,
    out_b,
    a_cat,
    pan,
    full,
    mt,
    xt,
    gt,
    part,
    fromp,
    total,
    rs,
    a_sem,
    pan_sem,
    g_send,
    g_recv,
    p_send,
    p_recv,
    r_send,
    r_recv,
):
    me_r, me_c, me_p = (lax.axis_index(name) for name in ("row", "col", "pole"))
    other = 1 - me_p
    tile_rows, tile_cols = ainv.shape[2], ainv.shape[3]
    width = tri_a.shape[2]
    share = tile_rows // ncol
    chunk = tile_rows // CHUNKS
    per_chunk = ncol // CHUNKS
    panels, marks, outs = (panel_a, panel_b), (rows_a, rows_b), (out_a, out_b)

    pan_copies = [
        pltpu.make_async_copy(panels[s].at[0], pan.at[s], pan_sem.at[s]) for s in range(2)
    ]
    a_copies = [
        pltpu.make_async_copy(
            ainv.at[0, d], a_cat.at[:, d * tile_cols : (d + 1) * tile_cols], a_sem.at[d]
        )
        for d in range(2)
    ]
    for copy in pan_copies + a_copies:
        copy.start()

    barrier = pltpu.get_barrier_semaphore()

    def greet(name, index, size):
        @pl.loop(1, size)
        def _(i):
            pl.semaphore_signal(
                barrier,
                inc=1,
                device_id={name: lax.rem(index + i, size)},
                device_id_type=MESH,
            )

    greet("row", me_r, nrow)
    greet("col", me_c, ncol)
    pl.semaphore_signal(barrier, inc=1, device_id={"pole": other}, device_id_type=MESH)

    for s in range(2):
        pan_copies[s].wait()
        keep = lane_marks(lambda j: marks[s][j], tile_cols // BS)
        full[s, me_r] = pan[s] * keep[None]

    pl.semaphore_wait(barrier, nrow + ncol - 1)

    def gather_copy(s, i):
        return remote(
            full.at[s, me_r],
            full.at[s, me_r],
            g_send.at[s, i],
            g_recv.at[s, i],
            {"row": lax.rem(me_r + i, nrow)},
        )

    for s in range(2):

        @pl.loop(1, nrow)
        def _(i):
            gather_copy(s, i).start()

    w_re, w_im = weights[0, 0], weights[0, 1]
    for s, tri in enumerate((tri_a, tri_b)):
        t_re, t_im = tri[0, 0].astype(jnp.float32), tri[0, 1].astype(jnp.float32)
        m_re = (w_im * t_im - w_re * t_re).T.astype(jnp.bfloat16)
        m_im = (-w_im * t_re - w_re * t_im).T.astype(jnp.bfloat16)
        mt[s, :width, :width] = m_im
        mt[s, :width, width:] = m_re
        mt[s, width:, :width] = m_re
        mt[s, width:, width:] = -m_im

    def mul(a, b):
        return jnp.dot(a, b, preferred_element_type=jnp.float32)

    x_re = (mul(cross[0, 0], tri_b[0, 0]) - mul(cross[0, 1], tri_b[0, 1])).T.astype(jnp.bfloat16)
    x_im = (mul(cross[0, 0], tri_b[0, 1]) + mul(cross[0, 1], tri_b[0, 0])).T.astype(jnp.bfloat16)
    xt[:width, :width] = -x_re
    xt[:width, width:] = -x_im
    xt[width:, :width] = x_im
    xt[width:, width:] = -x_re

    for copy in a_copies:
        copy.wait()

    @pl.loop(0, tile_rows // BS)
    def _(b):
        rows = pl.ds(pl.multiple_of(b * BS, BS), BS)
        keep = lane_marks(lambda j: pattern[j, b], tile_cols // BS)
        for d in range(2):
            columns = slice(d * tile_cols, (d + 1) * tile_cols)
            a_cat[rows, columns] = a_cat[rows, columns] * keep

    def pole_copy(s, q):
        rows = pl.ds(pl.multiple_of(q * chunk, chunk), chunk)
        return remote(
            part.at[s, other, rows],
            fromp.at[s, rows],
            p_send.at[s, q],
            p_recv.at[s, q],
            {"pole": other},
        )

    def sum_copy(s, i):
        to = lax.rem(me_c + i, ncol)
        return remote(
            total.at[s, to], rs.at[s, me_c], r_send.at[s, i], r_recv.at[s, i], {"col": to}
        )

    for s in range(2):

        @pl.loop(1, nrow)
        def _(i):
            gather_copy(s, i).wait_recv()

        for half in range(2):
            o_rows = slice(half * width, (half + 1) * width)
            lower = [full[s, :, d].reshape(width, tile_cols) for d in range(2)]
            g = mul(mt[s, o_rows, :width], lower[0]) + mul(mt[s, o_rows, width:], lower[1])
            if s == 1:
                g += mul(xt[o_rows, :width], gt[0, :, :tile_cols])
                g += mul(xt[o_rows, width:], gt[0, :, tile_cols:])
            gt[s, :, half * tile_cols : (half + 1) * tile_cols] = g.astype(jnp.bfloat16)

        first = lax.div(me_c, per_chunk)

        @pl.loop(0, CHUNKS)
        def _(n):
            q = lax.rem(first + 1 + n, CHUNKS)
            rows = pl.ds(pl.multiple_of(q * chunk, chunk), chunk)
            c = lax.dot_general(a_cat[rows, :], gt[s], NT, preferred_element_type=jnp.float32)
            c = c.astype(jnp.bfloat16)
            part[s, 0, rows] = c[:, :BS]
            part[s, 1, rows] = c[:, BS:]
            pole_copy(s, q).start()

        @pl.loop(0, CHUNKS)
        def _(n):
            q = lax.rem(first + 1 + n, CHUNKS)
            rows = pl.ds(pl.multiple_of(q * chunk, chunk), chunk)
            pole_copy(s, q).wait_recv()
            both = part[s, me_p, rows].astype(jnp.float32) + fromp[s, rows].astype(jnp.float32)
            total[s, pl.ds(q * per_chunk, per_chunk)] = both.astype(jnp.bfloat16).reshape(
                per_chunk, share, BS
            )

        @pl.loop(1, ncol)
        def _(i):
            sum_copy(s, i).start()

    for s in range(2):

        def add(i, acc):
            sum_copy(s, i).wait_recv()
            frm = lax.rem(me_c - i + ncol, ncol)
            return acc + rs[s, frm].astype(jnp.float32)

        outs[s][...] = lax.fori_loop(1, ncol, add, total[s, me_c].astype(jnp.float32))

    for s in range(2):

        @pl.loop(1, nrow)
        def _(i):
            gather_copy(s, i).wait_send()

        @pl.loop(0, CHUNKS)
        def _(q):
            pole_copy(s, q).wait_send()

        @pl.loop(1, ncol)
        def _(i):
            sum_copy(s, i).wait_send()


def solution(mesh):
    nrow, ncol = mesh.shape["row"], mesh.shape["col"]

    def per_device(
        ainv, pattern, rows_a, rows_b, panel_a, panel_b, tri_a, tri_b, cross_b, weights
    ):
        tile_rows, tile_cols = ainv.shape[2:]
        width, own_width = tri_a.shape[2], panel_a.shape[2]
        share = tile_rows // ncol
        anywhere = pl.BlockSpec(memory_space=pl.ANY)
        scalars = pl.BlockSpec(memory_space=pltpu.SMEM)
        whole = pl.BlockSpec(memory_space=pltpu.VMEM)
        bf16 = jnp.bfloat16
        dma = pltpu.SemaphoreType.DMA
        return pl.pallas_call(
            functools.partial(kernel, nrow, ncol),
            out_shape=[jax.ShapeDtypeStruct((share, BS), jnp.float32)] * 2,
            in_specs=[anywhere]
            + [scalars] * 3
            + [anywhere] * 2
            + [whole] * 3
            + [scalars],
            out_specs=[whole] * 2,
            scratch_shapes=[
                pltpu.VMEM((tile_rows, 2 * tile_cols), bf16),
                pltpu.VMEM((2, 2, own_width, tile_cols), bf16),
                pltpu.VMEM((2, nrow, 2, own_width, tile_cols), bf16),
                pltpu.VMEM((2, 2 * width, 2 * width), bf16),
                pltpu.VMEM((2 * width, 2 * width), bf16),
                pltpu.VMEM((2, width, 2 * tile_cols), bf16),
                pltpu.VMEM((2, 2, tile_rows, BS), bf16),
                pltpu.VMEM((2, tile_rows, BS), bf16),
                pltpu.VMEM((2, ncol, share, BS), bf16),
                pltpu.VMEM((2, ncol, share, BS), bf16),
                dma((2,)),
                dma((2,)),
                dma((2, nrow)),
                dma((2, nrow)),
                dma((2, CHUNKS)),
                dma((2, CHUNKS)),
                dma((2, ncol)),
                dma((2, ncol)),
            ],
            compiler_params=pltpu.CompilerParams(
                collective_id=0, has_side_effects=True, vmem_limit_bytes=56 << 20
            ),
        )(ainv, pattern.T, rows_a, rows_b, panel_a, panel_b, tri_a, tri_b, cross_b, weights)

    placed = (
        P("pole", None, "row", "col"),
        P("row", "col"),
        P("col"),
        P("col"),
        P("pole", None, "row", "col"),
        P("pole", None, "row", "col"),
        P("pole", None, None, None),
        P("pole", None, None, None),
        P("pole", None, None, None),
        P("pole", None),
    )
    return jax.shard_map(
        per_device,
        mesh=mesh,
        in_specs=placed,
        out_specs=(P(("row", "col"), "pole"), P(("row", "col"), "pole")),
        check_vma=False,
    )
```

time: 499 us -> 53 us (0.11)
  waiting for transfers between devices: 411 us -> 0 us
  Pallas kernels: 0 us -> 49.3 us
  blocking collectives: 48.7 us -> 0 us
  between operations: 14 us -> 0.64 us
  matrix products: 9.06 us -> 0 us
  local copies, waits for them, and re-layouts: 10.5 us -> 2.8 us
    reduce_scatter x2 -> x0, waiting for transfers between devices: 380 us -> none  [the longest x1 206 us: per_device(): lax.psum_scatter(block_product(masked, pair_b, out_rows * lax.axis_size('...]
    pallas_call x0 -> x1, Pallas kernels: none -> 49.3 us  [per_device(): pl.pallas_call(functools.partial(kernel, nrow, ncol), out_shape=[jax.Shap...]
    all_gather x2 -> x0, blocking collectives: 48.7 us -> none  [the longest x1 24.9 us: per_device(): lax.all_gather(lower_a, 'row', axis=1, tiled=True)]
    unnamed x6 -> x0, waiting for transfers between devices: 30.9 us -> none
    dot_general x6 -> x0, matrix products: 9.06 us -> none  [the longest x2 6.06 us: block_product(): jnp.einsum('crk,cdok->rdo', masked, pair, preferred_element_type=jnp.floa...]
    unnamed x29 -> x2, local copies, waits for them, and re-layouts: 9.2 us -> 2.8 us
  transfers between devices with their start and end apart: 4 -> 0, of which waited for: 4 -> 0; matrix products, arithmetic and copies ran while one was open for 2% -> 0% of each run, Pallas kernels for 0% -> 0%
where the time goes in v1:
time: 53 us; the launch traced here: 52.8 us
  Pallas kernels  49.3 us (93%)
  local copies, waits for them, and re-layouts  2.8 us (5%)
  between operations  0.64 us (1%)
    pallas_call x1, Pallas kernels, per_device(): pl.pallas_call(functools.partial(kernel, nrow, ncol), out_shape=[jax.Shap...  49.3 us
    unnamed x2, local copies, waits for them, and re-layouts  2.8 us

profile of v1, /device:TPU:1, one launch (start us, length us, event | category | flops | bytes accessed | tf_op | source)
XLA Modules:
  0.0 52.8 jit_solution(11357541511404135632)
XLA Ops:
  0.6 49.3 %shard_map.113 = (f32[80,128]{1,0:T(8,128)}, f32[80,128]{1,0:T(8,128)}) custom-call(bf16[1,2,1280,640]{3,2,1,0:T(8,128)(2,1)} %ainv.1, s32[5,10]{1,0:T(8,128)} %bitcast.1, s32[5]{0:T(128)} %rows_a.1, s32[5]{0:T(128)} %rows_b.1, bf16[1,2,32,640]{3,2,1,0:T(8,128)(2,1)} %panel_a.1, bf16[1,2,32,640]{3,2,1,0:T(8,128)(2,1)} %panel_b.1, ...), custom_call_target="tpu_custom_call" | custom-call | tf_op jit(solution)/shard_map/pallas_call | solution.py:252
  50.0 1.4 %copy.14 = f32[80,128]{1,0:T(8,128)} copy(f32[80,128]{1,0:T(8,128)} %get-tuple-element.4) | data formatting | bytes 81920
  51.4 1.4 %copy.15 = f32[80,128]{1,0:T(8,128)} copy(f32[80,128]{1,0:T(8,128)} %get-tuple-element.5) | data formatting | bytes 81920

commit v2 on v1

v2 whole, which is shorter than its diff:
```python
import functools

import jax
import jax.numpy as jnp
from jax import lax
from jax.experimental import pallas as pl
from jax.experimental.pallas import tpu as pltpu
from jax.sharding import PartitionSpec as P

BS = 128
CHUNKS = 4
LAG = 3
LATE = 1
MESH = pl.DeviceIdType.MESH
NT = (((1,), (1,)), ((), ()))


def remote(src, dst, send, recv, where):
    return pltpu.make_async_remote_copy(
        src_ref=src,
        dst_ref=dst,
        send_sem=send,
        recv_sem=recv,
        device_id=where,
        device_id_type=MESH,
    )


def lane_marks(marks, count):
    return jnp.concatenate(
        [jnp.full((1, BS), marks(j), jnp.int32) for j in range(count)], axis=1
    ).astype(jnp.float32).astype(jnp.bfloat16)


def spread(out, a_ref, b_ref):
    a_ref[...] = out[0]
    b_ref[...] = out[1]


def kernel(
    nrow,
    ncol,
    ainv,
    pattern,
    rows_a,
    rows_b,
    panel_a,
    panel_b,
    tri_a,
    tri_b,
    cross,
    weights,
    out,
    a_cat,
    pan,
    tri,
    full,
    mt,
    xt,
    gt,
    part,
    fromp,
    total,
    fromx,
    summed,
    rs,
    a_sem,
    pan_sem,
    tri_sem,
    g_send,
    g_recv,
    p_send,
    p_recv,
    x_send,
    x_recv,
    r_send,
    r_recv,
):
    me_r, me_c, me_p = (lax.axis_index(name) for name in ("row", "col", "pole"))
    other = 1 - me_p
    tile_rows, tile_cols = ainv.shape[2], ainv.shape[3]
    width = tri_a.shape[2]
    share = tile_rows // ncol
    chunk = tile_rows // CHUNKS
    per_chunk = ncol // CHUNKS
    ring = nrow // 2
    nz = ncol // 2
    me_z, me_h = lax.div(me_c, 2), lax.rem(me_c, 2)
    per_z = nz // CHUNKS

    def col_at(z, h):
        return z * 2 + h

    marks = (rows_a, rows_b)

    pan_copies = [
        pltpu.make_async_copy(ref.at[0], pan.at[s], pan_sem.at[s])
        for s, ref in enumerate((panel_a, panel_b))
    ]
    tri_copies = [
        pltpu.make_async_copy(ref.at[0], tri.at[s], tri_sem.at[s])
        for s, ref in enumerate((tri_a, tri_b, cross))
    ]
    a_copies = [
        pltpu.make_async_copy(
            ainv.at[0, d], a_cat.at[:, d * tile_cols : (d + 1) * tile_cols], a_sem.at[d]
        )
        for d in range(2)
    ]
    for copy in pan_copies:
        copy.start()

    def row_at(step):
        dx, dy = step
        x, y = lax.div(me_r, ring), lax.rem(me_r, ring)
        return lax.rem(x + dx, 2) * ring + lax.rem(y + dy + ring, ring)

    barrier = pltpu.get_barrier_semaphore()
    row_partners = ((0, 1), (0, -1), (0, 2), (1, 0))
    for step in row_partners:
        pl.semaphore_signal(
            barrier, inc=1, device_id={"row": row_at(step)}, device_id_type=MESH
        )
    pl.semaphore_signal(barrier, inc=1, device_id={"pole": other}, device_id_type=MESH)

    pl.semaphore_signal(
        barrier, inc=1, device_id={"col": col_at(me_z, 1 - me_h)}, device_id_type=MESH
    )

    @pl.loop(1, nz)
    def _(i):
        pl.semaphore_signal(
            barrier,
            inc=1,
            device_id={"col": col_at(lax.rem(me_z + i, nz), me_h)},
            device_id_type=MESH,
        )

    for copy in tri_copies + a_copies:
        copy.start()

    for s in range(2):
        pan_copies[s].wait()
        keep = lane_marks(lambda j: marks[s][j], tile_cols // BS)
        full[s, me_r] = pan[s] * keep[None]

    pl.semaphore_wait(barrier, len(row_partners) + nz + 1)

    hops = (
        ((0, 2), (0, 0), None),
        ((0, 1), (0, 0), None),
        ((0, -1), (0, 0), None),
        ((1, 0), (0, 0), None),
        ((0, 1), (1, 0), 3),
        ((0, -1), (1, 0), 3),
        ((1, 0), (0, 2), 0),
    )

    def gather_copy(s, i):
        to, owner, _ = hops[i]
        block = full.at[s, row_at(owner)]
        return remote(block, block, g_send.at[s, i], g_recv.at[s, i], {"row": row_at(to)})

    for s in range(2):
        for i in range(4):
            gather_copy(s, i).start()

    w_re, w_im = weights[0, 0], weights[0, 1]

    def scale(s):
        tri_copies[s].wait()
        t_re, t_im = tri[s, 0].astype(jnp.float32), tri[s, 1].astype(jnp.float32)
        m_re = (w_im * t_im - w_re * t_re).T.astype(jnp.bfloat16)
        m_im = (-w_im * t_re - w_re * t_im).T.astype(jnp.bfloat16)
        mt[s, :width, :width] = m_im
        mt[s, :width, width:] = m_re
        mt[s, width:, :width] = m_re
        mt[s, width:, width:] = -m_im

    scale(0)

    for s in range(2):
        gather_copy(s, 3).wait_recv()
        gather_copy(s, 4).start()
        gather_copy(s, 5).start()
        gather_copy(s, 0).wait_recv()
        gather_copy(s, 6).start()

    for copy in a_copies:
        copy.wait()

    @pl.loop(0, tile_rows // BS)
    def _(b):
        rows = pl.ds(pl.multiple_of(b * BS, BS), BS)
        keep = lane_marks(lambda j: pattern[j, b], tile_cols // BS)
        for d in range(2):
            columns = slice(d * tile_cols, (d + 1) * tile_cols)
            a_cat[rows, columns] = a_cat[rows, columns] * keep

    def mul(a, b):
        return jnp.dot(a, b, preferred_element_type=jnp.float32)

    def couple():
        tri_copies[2].wait()
        x_re = mul(tri[2, 0], tri[1, 0]) - mul(tri[2, 1], tri[1, 1])
        x_im = mul(tri[2, 0], tri[1, 1]) + mul(tri[2, 1], tri[1, 0])
        x_re, x_im = x_re.T.astype(jnp.bfloat16), x_im.T.astype(jnp.bfloat16)
        xt[:width, :width] = -x_re
        xt[:width, width:] = -x_im
        xt[width:, :width] = x_im
        xt[width:, width:] = -x_re

    scale(1)
    couple()

    def pole_copy(s, q):
        rows = pl.ds(pl.multiple_of(q * chunk, chunk), chunk)
        return remote(
            part.at[s, other, rows],
            fromp.at[s, rows],
            p_send.at[s, q],
            p_recv.at[s, q],
            {"pole": other},
        )

    def x_copy(s, q):
        shares = pl.ds(q * per_z, per_z)
        return remote(
            total.at[s, 1 - me_h, shares],
            fromx.at[s, shares],
            x_send.at[s, q],
            x_recv.at[s, q],
            {"col": col_at(me_z, 1 - me_h)},
        )

    def send_copy(s, to):
        return remote(
            summed.at[s, to],
            rs.at[s, me_z],
            r_send.at[s, to],
            r_recv.at[s, me_z],
            {"col": col_at(to, me_h)},
        )

    def take_copy(s, frm):
        return remote(
            summed.at[s, me_z],
            rs.at[s, frm],
            r_send.at[s, me_z],
            r_recv.at[s, frm],
            {"col": col_at(frm, me_h)},
        )

    first = lax.div(me_c, per_chunk)

    def turn(n):
        off = jnp.where(n == 0, 2, jnp.where(n == 1, 1, jnp.where(n == 2, 3, 0)))
        return lax.rem(first + off, CHUNKS)

    def pass_on(s):
        @pl.loop(0, CHUNKS)
        def _(n):
            q = turn(n)
            x_copy(s, q).wait_recv()
            shares = pl.ds(q * per_z, per_z)
            summed[s, shares] = (
                total[s, me_h, shares].astype(jnp.float32) + fromx[s, shares].astype(jnp.float32)
            ).astype(jnp.bfloat16)
            for j in range(per_z):
                to = q * per_z + j

                @pl.when(to != me_z)
                def _():
                    send_copy(s, to).start()

    for s in range(2):
        for i in (1, 2, 4, 5, 6):
            gather_copy(s, i).wait_recv()

        for half in range(2):
            o_rows = slice(half * width, (half + 1) * width)
            lower = [full[s, :, d].reshape(width, tile_cols) for d in range(2)]
            g = mul(mt[s, o_rows, :width], lower[0]) + mul(mt[s, o_rows, width:], lower[1])
            if s == 1:
                g += mul(xt[o_rows, :width], gt[0, :, :tile_cols])
                g += mul(xt[o_rows, width:], gt[0, :, tile_cols:])
            gt[s, :, half * tile_cols : (half + 1) * tile_cols] = g.astype(jnp.bfloat16)

        @pl.loop(0, CHUNKS + LAG)
        def _(n):
            @pl.when(n < CHUNKS)
            def _():
                q = turn(n)
                rows = pl.ds(pl.multiple_of(q * chunk, chunk), chunk)
                c = lax.dot_general(
                    a_cat[rows, :], gt[s], NT, preferred_element_type=jnp.float32
                ).astype(jnp.bfloat16)
                part[s, 0, rows] = c[:, :BS]
                part[s, 1, rows] = c[:, BS:]
                pole_copy(s, q).start()

            @pl.when(n >= LAG)
            def _():
                q = turn(n - LAG)
                rows = pl.ds(pl.multiple_of(q * chunk, chunk), chunk)
                pole_copy(s, q).wait_recv()
                both = part[s, me_p, rows].astype(jnp.float32) + fromp[s, rows].astype(jnp.float32)
                both = both.astype(jnp.bfloat16).reshape(per_z, 2, share, BS)
                for h in range(2):
                    for j in range(per_z):
                        total[s, h, q * per_z + j] = both[j, h]
                x_copy(s, q).start()

        if s >= LATE:
            for late in range(s - LATE, s + 1 if s == 1 else s - LATE + 1):
                pass_on(late)

    for s in range(2):

        def add(i, acc):
            frm = lax.rem(me_z + i, nz)
            take_copy(s, frm).wait_recv()
            return acc + rs[s, frm].astype(jnp.float32)

        out[s] = lax.fori_loop(1, nz, add, summed[s, me_z].astype(jnp.float32))

    for s in range(2):
        for i in range(len(hops)):
            gather_copy(s, i).wait_send()

        @pl.loop(0, CHUNKS)
        def _(q):
            pole_copy(s, q).wait_send()
            x_copy(s, q).wait_send()

        @pl.loop(1, nz)
        def _(i):
            send_copy(s, lax.rem(me_z + i, nz)).wait_send()


def solution(mesh):
    nrow, ncol = mesh.shape["row"], mesh.shape["col"]

    def per_device(
        ainv, pattern, rows_a, rows_b, panel_a, panel_b, tri_a, tri_b, cross_b, weights
    ):
        tile_rows, tile_cols = ainv.shape[2:]
        width, own_width = tri_a.shape[2], panel_a.shape[2]
        share = tile_rows // ncol
        anywhere = pl.BlockSpec(memory_space=pl.ANY)
        scalars = pl.BlockSpec(memory_space=pltpu.SMEM)
        whole = pl.BlockSpec(memory_space=pltpu.VMEM)
        bf16 = jnp.bfloat16
        dma = pltpu.SemaphoreType.DMA
        dens = pl.pallas_call(
            functools.partial(kernel, nrow, ncol),
            out_shape=jax.ShapeDtypeStruct((2, share, BS), jnp.float32),
            in_specs=[anywhere] + [scalars] * 3 + [anywhere] * 5 + [scalars],
            out_specs=whole,
            scratch_shapes=[
                pltpu.VMEM((tile_rows, 2 * tile_cols), bf16),
                pltpu.VMEM((2, 2, own_width, tile_cols), bf16),
                pltpu.VMEM((3, 2, width, width), bf16),
                pltpu.VMEM((2, nrow, 2, own_width, tile_cols), bf16),
                pltpu.VMEM((2, 2 * width, 2 * width), bf16),
                pltpu.VMEM((2 * width, 2 * width), bf16),
                pltpu.VMEM((2, width, 2 * tile_cols), bf16),
                pltpu.VMEM((2, 2, tile_rows, BS), bf16),
                pltpu.VMEM((2, tile_rows, BS), bf16),
                pltpu.VMEM((2, 2, ncol // 2, share, BS), bf16),
                pltpu.VMEM((2, ncol // 2, share, BS), bf16),
                pltpu.VMEM((2, ncol // 2, share, BS), bf16),
                pltpu.VMEM((2, ncol // 2, share, BS), bf16),
                dma((2,)),
                dma((2,)),
                dma((3,)),
                dma((2, 7)),
                dma((2, 7)),
                dma((2, CHUNKS)),
                dma((2, CHUNKS)),
                dma((2, CHUNKS)),
                dma((2, CHUNKS)),
                dma((2, ncol // 2)),
                dma((2, ncol // 2)),
            ],
            compiler_params=pltpu.CompilerParams(
                collective_id=0, has_side_effects=True, vmem_limit_bytes=56 << 20
            ),
        )(ainv, pattern.T, rows_a, rows_b, panel_a, panel_b, tri_a, tri_b, cross_b, weights)
        return pl.pallas_call(
            spread,
            out_shape=[jax.ShapeDtypeStruct((share, BS), jnp.float32)] * 2,
            in_specs=[whole],
            out_specs=[whole] * 2,
        )(dens)

    placed = (
        P("pole", None, "row", "col"),
        P("row", "col"),
        P("col"),
        P("col"),
        P("pole", None, "row", "col"),
        P("pole", None, "row", "col"),
        P("pole", None, None, None),
        P("pole", None, None, None),
        P("pole", None, None, None),
        P("pole", None),
    )
    return jax.shard_map(
        per_device,
        mesh=mesh,
        in_specs=placed,
        out_specs=(P(("row", "col"), "pole"), P(("row", "col"), "pole")),
        check_vma=False,
    )
```

time: 53 us -> 42.5 us (0.80)
  Pallas kernels: 49.3 us -> 41.7 us
  local copies, waits for them, and re-layouts: 2.8 us -> 0 us
    pallas_call x1 -> x2, Pallas kernels: 49.3 us -> 41.7 us  [the longest x1 40.2 us: per_device(): pl.pallas_call(functools.partial(kernel, nrow, ncol), out_shape=jax.Shape...]
    unnamed x2 -> x0, local copies, waits for them, and re-layouts: 2.8 us -> none
where the time goes in v2:
time: 42.5 us; the launch traced here: 42.3 us
  Pallas kernels  41.7 us (98%)
  between operations  0.64 us (2%)
    pallas_call x1, Pallas kernels, per_device(): pl.pallas_call(functools.partial(kernel, nrow, ncol), out_shape=jax.Shape...  40.2 us
    pallas_call x1, Pallas kernels, per_device(): pl.pallas_call(spread, out_shape=[jax.ShapeDtypeStruct((share, BS), jnp.f...  1.52 us

profile of v2, /device:TPU:1, one launch (start us, length us, event | category | flops | bytes accessed | tf_op | source)
XLA Modules:
  0.0 42.3 jit_solution(4008224082103362694)
XLA Ops:
  0.6 40.2 %shard_map.113.out = f32[2,80,128]{2,1,0:T(8,128)} custom-call(bf16[1,2,1280,640]{3,2,1,0:T(8,128)(2,1)} %ainv.1, s32[5,10]{1,0:T(8,128)} %bitcast.1, s32[5]{0:T(128)} %rows_a.1, s32[5]{0:T(128)} %rows_b.1, bf16[1,2,32,640]{3,2,1,0:T(8,128)(2,1)} %panel_a.1, bf16[1,2,32,640]{3,2,1,0:T(8,128)(2,1)} %panel_b.1, bf16[1,2,256,256]{3,2,1,0:T(8,128)(2,1)} %tri_a.1, ...), custom_call_target="tpu_custom_call" | custom-call | tf_op jit(solution)/shard_map/pallas_call | solution.py:355
  40.8 1.5 %shard_map.114 = (f32[80,128]{1,0:T(8,128)}, f32[80,128]{1,0:T(8,128)}) custom-call(f32[2,80,128]{2,1,0:T(8,128)} %shard_map.113.out), custom_call_target="tpu_custom_call" | custom-call | tf_op jit(solution)/shard_map/pallas_call | solution.py:390

commit v3 on v2

--- a/solution.py
+++ b/solution.py
@@ -9,8 +9,6 @@
 
 BS = 128
 CHUNKS = 4
-LAG = 3
-LATE = 1
 MESH = pl.DeviceIdType.MESH
 NT = (((1,), (1,)), ((), ()))
 
@@ -58,6 +56,7 @@
     mt,
     xt,
     gt,
+    coupled,
     part,
     fromp,
     total,
@@ -75,6 +74,7 @@
     x_recv,
     r_send,
     r_recv,
+    in_sem,
 ):
     me_r, me_c, me_p = (lax.axis_index(name) for name in ("row", "col", "pole"))
     other = 1 - me_p
@@ -127,14 +127,11 @@
         barrier, inc=1, device_id={"col": col_at(me_z, 1 - me_h)}, device_id_type=MESH
     )
 
-    @pl.loop(1, nz)
-    def _(i):
-        pl.semaphore_signal(
-            barrier,
-            inc=1,
-            device_id={"col": col_at(lax.rem(me_z + i, nz), me_h)},
-            device_id_type=MESH,
-        )
+    def along_z(step):
+        return {"col": col_at(lax.rem(me_z + step + nz, nz), me_h)}
+
+    for step in (1, -1):
+        pl.semaphore_signal(barrier, inc=1, device_id=along_z(step), device_id_type=MESH)
 
     for copy in tri_copies + a_copies:
         copy.start()
@@ -144,26 +141,45 @@
         keep = lane_marks(lambda j: marks[s][j], tile_cols // BS)
         full[s, me_r] = pan[s] * keep[None]
 
-    pl.semaphore_wait(barrier, len(row_partners) + nz + 1)
-
-    hops = (
-        ((0, 2), (0, 0), None),
-        ((0, 1), (0, 0), None),
-        ((0, -1), (0, 0), None),
-        ((1, 0), (0, 0), None),
-        ((0, 1), (1, 0), 3),
-        ((0, -1), (1, 0), 3),
-        ((1, 0), (0, 2), 0),
-    )
+    pl.semaphore_wait(barrier, len(row_partners) + 4)
+
+    hops = ((((1,0),(0,0),None,None),((0,2),(0,0),None,None),((0,1),(0,0),None,None),((0,-1),(0,0),None,None),((0,1),(1,0),None,0),((0,-1),(1,0),None,0),((1,0),(0,2),None,1)), (((1,0),(0,0),None,None),((0,2),(0,0),None,None),((0,1),(0,0),None,None),((0,-1),(0,0),None,None),((0,1),(1,0),None,0),((0,-1),(1,0),None,0),((1,0),(0,2),None,1)))
 
     def gather_copy(s, i):
-        to, owner, _ = hops[i]
+        to, owner, part_of, _ = hops[s][i]
         block = full.at[s, row_at(owner)]
+        if part_of is not None:
+            block = block.at[part_of]
         return remote(block, block, g_send.at[s, i], g_recv.at[s, i], {"row": row_at(to)})
 
-    for s in range(2):
-        for i in range(4):
+    arrived = set()
+
+    def arrive(s, i):
+        if (s, i) not in arrived:
+            arrived.add((s, i))
+            gather_copy(s, i).wait_recv()
+
+    def pass_blocks(order):
+        for s, i in order:
+            if hops[s][i][3] is not None:
+                arrive(s, hops[s][i][3])
             gather_copy(s, i).start()
+
+    def tell(turn_of):
+        for side, step in enumerate((1, -1)):
+            pl.semaphore_signal(
+                in_sem.at[turn_of, side],
+                inc=1,
+                device_id=along_z(step * (turn_of + 1)),
+                device_id_type=MESH,
+            )
+
+    def hear(turn_of):
+        for side in range(2):
+            pl.semaphore_wait(in_sem.at[turn_of, side], 1)
+
+    tell(0)
+    pass_blocks(((0, 0), (0, 1), (1, 0), (1, 1), (0, 2), (0, 3), (1, 2), (1, 3)))
 
     w_re, w_im = weights[0, 0], weights[0, 1]
 
@@ -177,14 +193,11 @@
         mt[s, width:, :width] = m_re
         mt[s, width:, width:] = -m_im
 
+    hear(0)
+    tell(1)
     scale(0)
 
-    for s in range(2):
-        gather_copy(s, 3).wait_recv()
-        gather_copy(s, 4).start()
-        gather_copy(s, 5).start()
-        gather_copy(s, 0).wait_recv()
-        gather_copy(s, 6).start()
+    pass_blocks(((0, 4), (0, 5), (0, 6), (1, 4), (1, 5), (1, 6)))
 
     for copy in a_copies:
         copy.wait()
@@ -212,6 +225,7 @@
 
     scale(1)
     couple()
+    hear(1)
 
     def pole_copy(s, q):
         rows = pl.ds(pl.multiple_of(q * chunk, chunk), chunk)
@@ -254,7 +268,7 @@
     first = lax.div(me_c, per_chunk)
 
     def turn(n):
-        off = jnp.where(n == 0, 2, jnp.where(n == 1, 1, jnp.where(n == 2, 3, 0)))
+        off = CHUNKS // 2 + lax.div(n + 1, 2) * (1 - 2 * lax.rem(n, 2))
         return lax.rem(first + off, CHUNKS)
 
     def pass_on(s):
@@ -274,46 +288,49 @@
                     send_copy(s, to).start()
 
     for s in range(2):
-        for i in (1, 2, 4, 5, 6):
-            gather_copy(s, i).wait_recv()
+        for i in range(len(hops[s])):
+            arrive(s, i)
 
         for half in range(2):
             o_rows = slice(half * width, (half + 1) * width)
             lower = [full[s, :, d].reshape(width, tile_cols) for d in range(2)]
             g = mul(mt[s, o_rows, :width], lower[0]) + mul(mt[s, o_rows, width:], lower[1])
             if s == 1:
-                g += mul(xt[o_rows, :width], gt[0, :, :tile_cols])
-                g += mul(xt[o_rows, width:], gt[0, :, tile_cols:])
+                g += coupled[half]
             gt[s, :, half * tile_cols : (half + 1) * tile_cols] = g.astype(jnp.bfloat16)
 
-        @pl.loop(0, CHUNKS + LAG)
+        @pl.loop(0, CHUNKS)
         def _(n):
-            @pl.when(n < CHUNKS)
-            def _():
-                q = turn(n)
-                rows = pl.ds(pl.multiple_of(q * chunk, chunk), chunk)
-                c = lax.dot_general(
-                    a_cat[rows, :], gt[s], NT, preferred_element_type=jnp.float32
-                ).astype(jnp.bfloat16)
-                part[s, 0, rows] = c[:, :BS]
-                part[s, 1, rows] = c[:, BS:]
-                pole_copy(s, q).start()
-
-            @pl.when(n >= LAG)
-            def _():
-                q = turn(n - LAG)
-                rows = pl.ds(pl.multiple_of(q * chunk, chunk), chunk)
-                pole_copy(s, q).wait_recv()
-                both = part[s, me_p, rows].astype(jnp.float32) + fromp[s, rows].astype(jnp.float32)
-                both = both.astype(jnp.bfloat16).reshape(per_z, 2, share, BS)
-                for h in range(2):
-                    for j in range(per_z):
-                        total[s, h, q * per_z + j] = both[j, h]
-                x_copy(s, q).start()
-
-        if s >= LATE:
-            for late in range(s - LATE, s + 1 if s == 1 else s - LATE + 1):
-                pass_on(late)
+            q = turn(n)
+            rows = pl.ds(pl.multiple_of(q * chunk, chunk), chunk)
+            c = lax.dot_general(
+                a_cat[rows, :], gt[s], NT, preferred_element_type=jnp.float32
+            ).astype(jnp.bfloat16)
+            part[s, 0, rows] = c[:, :BS]
+            part[s, 1, rows] = c[:, BS:]
+            pole_copy(s, q).start()
+
+        if s == 0:
+            for half in range(2):
+                o_rows = slice(half * width, (half + 1) * width)
+                coupled[half] = mul(xt[o_rows, :width], gt[0, :, :tile_cols]) + mul(
+                    xt[o_rows, width:], gt[0, :, tile_cols:]
+                )
+
+        @pl.loop(0, CHUNKS)
+        def _(n):
+            q = turn(n)
+            rows = pl.ds(pl.multiple_of(q * chunk, chunk), chunk)
+            pole_copy(s, q).wait_recv()
+            both = part[s, me_p, rows].astype(jnp.float32) + fromp[s, rows].astype(jnp.float32)
+            both = both.astype(jnp.bfloat16).reshape(per_z, 2, share, BS)
+            for h in range(2):
+                for j in range(per_z):
+                    total[s, h, q * per_z + j] = both[j, h]
+            x_copy(s, q).start()
+
+    for s in range(2):
+        pass_on(s)
 
     for s in range(2):
 
@@ -325,7 +342,7 @@
         out[s] = lax.fori_loop(1, nz, add, summed[s, me_z].astype(jnp.float32))
 
     for s in range(2):
-        for i in range(len(hops)):
+        for i in range(len(hops[s])):
             gather_copy(s, i).wait_send()
 
         @pl.loop(0, CHUNKS)
@@ -365,6 +382,7 @@
                 pltpu.VMEM((2, 2 * width, 2 * width), bf16),
                 pltpu.VMEM((2 * width, 2 * width), bf16),
                 pltpu.VMEM((2, width, 2 * tile_cols), bf16),
+                pltpu.VMEM((2, width, tile_cols), jnp.float32),
                 pltpu.VMEM((2, 2, tile_rows, BS), bf16),
                 pltpu.VMEM((2, tile_rows, BS), bf16),
                 pltpu.VMEM((2, 2, ncol // 2, share, BS), bf16),
@@ -374,14 +392,15 @@
                 dma((2,)),
                 dma((2,)),
                 dma((3,)),
-                dma((2, 7)),
-                dma((2, 7)),
+                dma((2, 10)),
+                dma((2, 10)),
                 dma((2, CHUNKS)),
                 dma((2, CHUNKS)),
                 dma((2, CHUNKS)),
                 dma((2, CHUNKS)),
                 dma((2, ncol // 2)),
                 dma((2, ncol // 2)),
+                pltpu.SemaphoreType.REGULAR((2, 2)),
             ],
             compiler_params=pltpu.CompilerParams(
                 collective_id=0, has_side_effects=True, vmem_limit_bytes=56 << 20

time: 42.5 us -> 40.5 us (0.953)
  Pallas kernels: 41.7 us -> 39.4 us
    pallas_call x1, Pallas kernels: 40.2 us -> 37.9 us  [per_device(): pl.pallas_call(functools.partial(kernel, nrow, ncol), out_shape=jax.Shape...]
where the time goes in v3:
time: 40.5 us; the launch traced here: 40.1 us
  Pallas kernels  39.4 us (97%)
  between operations  0.64 us (2%)
    pallas_call x1, Pallas kernels, per_device(): pl.pallas_call(functools.partial(kernel, nrow, ncol), out_shape=jax.Shape...  37.9 us
    pallas_call x1, Pallas kernels, per_device(): pl.pallas_call(spread, out_shape=[jax.ShapeDtypeStruct((share, BS), jnp.f...  1.52 us

profile of v3, /device:TPU:1, one launch (start us, length us, event | category | flops | bytes accessed | tf_op | source)
XLA Modules:
  0.0 40.1 jit_solution(11983329010087132246)
XLA Ops:
  0.6 37.9 %shard_map.113.out = f32[2,80,128]{2,1,0:T(8,128)} custom-call(bf16[1,2,1280,640]{3,2,1,0:T(8,128)(2,1)} %ainv.1, s32[5,10]{1,0:T(8,128)} %bitcast.1, s32[5]{0:T(128)} %rows_a.1, s32[5]{0:T(128)} %rows_b.1, bf16[1,2,32,640]{3,2,1,0:T(8,128)(2,1)} %panel_a.1, bf16[1,2,32,640]{3,2,1,0:T(8,128)(2,1)} %panel_b.1, bf16[1,2,256,256]{3,2,1,0:T(8,128)(2,1)} %tri_a.1, ...), custom_call_target="tpu_custom_call" | custom-call | tf_op jit(solution)/shard_map/pallas_call | solution.py:372
  38.5 1.5 %shard_map.114 = (f32[80,128]{1,0:T(8,128)}, f32[80,128]{1,0:T(8,128)}) custom-call(f32[2,80,128]{2,1,0:T(8,128)} %shard_map.113.out), custom_call_target="tpu_custom_call" | custom-call | tf_op jit(solution)/shard_map/pallas_call | solution.py:409

commit v4 on v3

--- a/solution.py
+++ b/solution.py
@@ -28,11 +28,6 @@
     return jnp.concatenate(
         [jnp.full((1, BS), marks(j), jnp.int32) for j in range(count)], axis=1
     ).astype(jnp.float32).astype(jnp.bfloat16)
-
-
-def spread(out, a_ref, b_ref):
-    a_ref[...] = out[0]
-    b_ref[...] = out[1]
 
 
 def kernel(
@@ -333,6 +328,15 @@
         pass_on(s)
 
     for s in range(2):
+        for i in range(len(hops[s])):
+            gather_copy(s, i).wait_send()
+
+        @pl.loop(0, CHUNKS)
+        def _(q):
+            pole_copy(s, q).wait_send()
+            x_copy(s, q).wait_send()
+
+    for s in range(2):
 
         def add(i, acc):
             frm = lax.rem(me_z + i, nz)
@@ -342,13 +346,6 @@
         out[s] = lax.fori_loop(1, nz, add, summed[s, me_z].astype(jnp.float32))
 
     for s in range(2):
-        for i in range(len(hops[s])):
-            gather_copy(s, i).wait_send()
-
-        @pl.loop(0, CHUNKS)
-        def _(q):
-            pole_copy(s, q).wait_send()
-            x_copy(s, q).wait_send()
 
         @pl.loop(1, nz)
         def _(i):
@@ -371,7 +368,7 @@
         dma = pltpu.SemaphoreType.DMA
         dens = pl.pallas_call(
             functools.partial(kernel, nrow, ncol),
-            out_shape=jax.ShapeDtypeStruct((2, share, BS), jnp.float32),
+            out_shape=pltpu.VMEM((2, share, BS), jnp.float32),
             in_specs=[anywhere] + [scalars] * 3 + [anywhere] * 5 + [scalars],
             out_specs=whole,
             scratch_shapes=[
@@ -406,12 +403,7 @@
                 collective_id=0, has_side_effects=True, vmem_limit_bytes=56 << 20
             ),
         )(ainv, pattern.T, rows_a, rows_b, panel_a, panel_b, tri_a, tri_b, cross_b, weights)
-        return pl.pallas_call(
-            spread,
-            out_shape=[jax.ShapeDtypeStruct((share, BS), jnp.float32)] * 2,
-            in_specs=[whole],
-            out_specs=[whole] * 2,
-        )(dens)
+        return dens[0], dens[1]
 
     placed = (
         P("pole", None, "row", "col"),

time: 40.5 us -> 38.9 us (0.960)
  Pallas kernels: 39.4 us -> 37.5 us
  local copies, waits for them, and re-layouts: 0 us -> 0.64 us
    pallas_call x2 -> x1, Pallas kernels: 39.4 us -> 37.5 us  [per_device(): pl.pallas_call(functools.partial(kernel, nrow, ncol), out_shape=pltpu.VME...]
    squeeze x0 -> x1, local copies, waits for them, and re-layouts: none -> 0.64 us  [per_device(): return (dens[0], dens[1])]
where the time goes in v4:
time: 38.9 us; the launch traced here: 38.8 us
  Pallas kernels  37.5 us (96%)
  local copies, waits for them, and re-layouts  0.64 us (2%)
  between operations  0.64 us (2%)
    pallas_call x1, Pallas kernels, per_device(): pl.pallas_call(functools.partial(kernel, nrow, ncol), out_shape=pltpu.VME...  37.5 us

profile of v4, /device:TPU:1, one launch (start us, length us, event | category | flops | bytes accessed | tf_op | source)
XLA Modules:
  0.0 38.8 jit_solution(245601973637992755)
XLA Ops:
  0.6 37.5 %shard_map.113 = f32[2,80,128]{2,1,0:T(8,128)S(1)} custom-call(bf16[1,2,1280,640]{3,2,1,0:T(8,128)(2,1)} %ainv.1, s32[5,10]{1,0:T(8,128)} %bitcast.5, s32[5]{0:T(128)} %rows_a.1, s32[5]{0:T(128)} %rows_b.1, bf16[1,2,32,640]{3,2,1,0:T(8,128)(2,1)} %panel_a.1, bf16[1,2,32,640]{3,2,1,0:T(8,128)(2,1)} %panel_b.1, bf16[1,2,256,256]{3,2,1,0:T(8,128)(2,1)} %tri_a.1, ...), custom_call_target="tpu_custom_call" | custom-call | tf_op jit(solution)/shard_map/pallas_call | solution.py:369
  38.2 0.6 %slice_bitcast_fusion = (f32[80,128]{1,0:T(8,128)}, f32[80,128]{1,0:T(8,128)}) fusion(f32[2,80,128]{2,1,0:T(8,128)S(1)} %shard_map.113), kind=kLoop, calls=%fused_computation | loop fusion | bytes 163840 | tf_op jit(solution)/shard_map/squeeze | solution.py:406

commit v5 on v4

--- a/solution.py
+++ b/solution.py
@@ -138,7 +138,7 @@
 
     pl.semaphore_wait(barrier, len(row_partners) + 4)
 
-    hops = ((((1,0),(0,0),None,None),((0,2),(0,0),None,None),((0,1),(0,0),None,None),((0,-1),(0,0),None,None),((0,1),(1,0),None,0),((0,-1),(1,0),None,0),((1,0),(0,2),None,1)), (((1,0),(0,0),None,None),((0,2),(0,0),None,None),((0,1),(0,0),None,None),((0,-1),(0,0),None,None),((0,1),(1,0),None,0),((0,-1),(1,0),None,0),((1,0),(0,2),None,1)))
+    hops = ((((1,0),(0,0),None,None),((0,2),(0,0),None,None),((0,1),(0,0),None,None),((0,-1),(0,0),None,None),((0,1),(1,0),None,0),((0,-1),(1,0),None,0),((1,0),(0,2),None,1)), (((1,0),(0,0),None,None),((0,2),(0,0),None,None),((0,1),(0,0),None,None),((0,-1),(0,0),None,None),((0,1),(1,0),1,0),((0,-1),(1,0),0,0),((1,0),(0,-1),0,2),((1,0),(0,1),1,3),((1,0),(0,2),None,1)))
 
     def gather_copy(s, i):
         to, owner, part_of, _ = hops[s][i]
@@ -188,12 +188,12 @@
         mt[s, width:, :width] = m_re
         mt[s, width:, width:] = -m_im
 
+    scale(0)
+
+    pass_blocks(((0, 4), (0, 5), (0, 6), (1, 4), (1, 5), (1, 8), (1, 6), (1, 7)))
+
     hear(0)
     tell(1)
-    scale(0)
-
-    pass_blocks(((0, 4), (0, 5), (0, 6), (1, 4), (1, 5), (1, 6)))
-
     for copy in a_copies:
         copy.wait()
 

time: 38.9 us -> 39.8 us (1.023)
  Pallas kernels: 37.5 us -> 38.4 us
    pallas_call x1, Pallas kernels: 37.5 us -> 38.4 us  [per_device(): pl.pallas_call(functools.partial(kernel, nrow, ncol), out_shape=pltpu.VME...]
where the time goes in v5:
time: 39.8 us; the launch traced here: 39.7 us
  Pallas kernels  38.4 us (96%)
  local copies, waits for them, and re-layouts  0.64 us (2%)
  between operations  0.64 us (2%)
    pallas_call x1, Pallas kernels, per_device(): pl.pallas_call(functools.partial(kernel, nrow, ncol), out_shape=pltpu.VME...  38.4 us

profile of v5, /device:TPU:1, one launch (start us, length us, event | category | flops | bytes accessed | tf_op | source)
XLA Modules:
  0.0 39.7 jit_solution(12716596741428558247)
XLA Ops:
  0.6 38.4 %shard_map.113 = f32[2,80,128]{2,1,0:T(8,128)S(1)} custom-call(bf16[1,2,1280,640]{3,2,1,0:T(8,128)(2,1)} %ainv.1, s32[5,10]{1,0:T(8,128)} %bitcast.5, s32[5]{0:T(128)} %rows_a.1, s32[5]{0:T(128)} %rows_b.1, bf16[1,2,32,640]{3,2,1,0:T(8,128)(2,1)} %panel_a.1, bf16[1,2,32,640]{3,2,1,0:T(8,128)(2,1)} %panel_b.1, bf16[1,2,256,256]{3,2,1,0:T(8,128)(2,1)} %tri_a.1, ...), custom_call_target="tpu_custom_call" | custom-call | tf_op jit(solution)/shard_map/pallas_call | solution.py:369
  39.0 0.6 %slice_bitcast_fusion = (f32[80,128]{1,0:T(8,128)}, f32[80,128]{1,0:T(8,128)}) fusion(f32[2,80,128]{2,1,0:T(8,128)S(1)} %shard_map.113), kind=kLoop, calls=%fused_computation | loop fusion | bytes 163840 | tf_op jit(solution)/shard_map/squeeze | solution.py:406
